TPU v7x, 256 devices: a whole 4x4x8 slice. The times are simulated.
256 devices in a mesh: dp: 4 (over y), seq: 64 (over z, x, core).
Axes of the slice: x: 4, y: 4, z: 8, core: 2. Of those that a mesh axis runs over, the one named last changes fastest.
Arguments:
- query: bfloat16 [4, 16384, 1536], P('dp', 'seq'), may hold values from -6 to 6
- key: bfloat16 [4, 16384, 1536], P('dp', 'seq'), may hold values from -6 to 6
- value: bfloat16 [4, 16384, 1536], P('dp', 'seq'), may hold values from -6 to 6
- segments: int32 [4, 16384], P('dp', 'seq'), may hold values from 0 to 95, never falling along the last dimension, each value on 1 to 256 neighbouring positions
- out_proj: bfloat16 [1536, 1536], replicated, may hold values from -0.15625 to 0.15625
- conv_kernel: bfloat16 [31, 1536], replicated, may hold values from -1 to 1
- cotangent: bfloat16 [4, 16384, 1536], P('dp', 'seq'), may hold values from -6 to 6
Outputs:
- block_out: bfloat16 [4, 16384, 1536], P('dp', 'seq')
- grad_query: bfloat16 [4, 16384, 1536], P('dp', 'seq')
- grad_key: bfloat16 [4, 16384, 1536], P('dp', 'seq')
- grad_value: bfloat16 [4, 16384, 1536], P('dp', 'seq')
- grad_kernel: float32 [31, 1536], replicated
- grad_out_proj: float32 [1536, 1536], P(('dp', 'seq'))
Inputs may be any that keep to these rules, and one draw needn't show every extreme that they name: `segments`: along the frames of a data group the utterance number never falls; every utterance holds 1 to 256 frames and one holds exactly 256.
All inputs are finite; a program needn't handle non-finite values.
Results may differ from a plain program's by a relative error of at most 0.02.
Values may be sent and summed in bfloat16 or wider, within the bound.
No kernel may reach another device: no remote copies, remote signals or barrier semaphores. Data moves between devices by JAX's collectives and lax.ppermute only.
A program may use at most 128 MiB of HBM per device.

v0:
```python
import jax
import jax.numpy as jnp
from jax import lax
from jax.sharding import PartitionSpec as P

HD = 64
KW = 31


def extended(block, sides, width):
    for axis, dim in sides:
        count = lax.axis_size(axis)
        forward = [(i, i + 1) for i in range(count - 1)]
        backward = [(target, source) for source, target in forward]
        low = lax.ppermute(
            lax.slice_in_dim(block, block.shape[dim] - width, None, axis=dim), axis, forward
        )
        high = lax.ppermute(lax.slice_in_dim(block, 0, width, axis=dim), axis, backward)
        block = jnp.concatenate([low, block, high], axis=dim)
    return block


def from_behind(value, axis, steps):
    count = lax.axis_size(axis)
    first, last = (max(0, -steps), min(count, count - steps))
    return lax.ppermute(value, axis, [(source, source + steps) for source in range(first, last)])


def head_scores(queries, keys_block, query_ids, key_ids):
    query_heads = queries.reshape(queries.shape[0], -1, HD)
    key_heads = keys_block.reshape(keys_block.shape[0], -1, HD)
    scores = jnp.einsum(
        "rhe,whe->hrw", query_heads, key_heads, preferred_element_type=jnp.float32
    ) * HD ** (-0.5)
    allowed = query_ids[:, None] == key_ids[None, :]
    return jnp.where(allowed[None], scores, -1e30)


def to_groups(matrix):
    return jnp.moveaxis(matrix.reshape(matrix.shape[0], -1, 4 * HD), 1, 0)


def from_groups(stacked):
    return jnp.moveaxis(stacked, 0, 1).reshape(stacked.shape[1], -1)


def attend(queries, keys_block, values_block, query_ids, key_ids):
    scores = head_scores(queries, keys_block, query_ids, key_ids)
    highest = jnp.max(scores, axis=2)
    weights = jnp.exp(scores - highest[:, :, None])
    totals = jnp.sum(weights, axis=2)
    probs = (weights / totals[:, :, None]).astype(jnp.bfloat16)
    value_heads = values_block.reshape(values_block.shape[0], -1, HD)
    context = jnp.einsum("hrw,whe->rhe", probs, value_heads, preferred_element_type=jnp.float32)
    return (context.reshape(queries.shape[0], -1), highest, totals)


def score_grads(
    queries, keys_block, values_block, upstream, highest, totals, deltas, query_ids, key_ids
):
    scores = head_scores(queries, keys_block, query_ids, key_ids)
    probs = jnp.exp(scores - highest[:, :, None]) / totals[:, :, None]
    upstream_heads = upstream.reshape(upstream.shape[0], -1, HD)
    value_heads = values_block.reshape(values_block.shape[0], -1, HD)
    prob_grads = jnp.einsum(
        "rhe,whe->hrw", upstream_heads, value_heads, preferred_element_type=jnp.float32
    )
    score_grad = (probs * (prob_grads - deltas[:, :, None]) * HD ** (-0.5)).astype(jnp.bfloat16)
    return (probs.astype(jnp.bfloat16), score_grad, upstream_heads)


def query_side(queries, keys_block, score_grad):
    key_heads = keys_block.reshape(keys_block.shape[0], -1, HD)
    grads = jnp.einsum("hrw,whe->rhe", score_grad, key_heads, preferred_element_type=jnp.float32)
    return grads.reshape(queries.shape[0], -1)


def key_side(queries, keys_block, probs, score_grad, upstream_heads):
    query_heads = queries.reshape(queries.shape[0], -1, HD)
    key_part = jnp.einsum(
        "hrw,rhe->whe", score_grad, query_heads, preferred_element_type=jnp.float32
    )
    value_part = jnp.einsum(
        "hrw,rhe->whe", probs, upstream_heads, preferred_element_type=jnp.float32
    )
    return (key_part.reshape(keys_block.shape[0], -1), value_part.reshape(keys_block.shape[0], -1))


def per_device(query, key, value, segments, out_proj, conv_kernel, cotangent):
    frame_count = query.shape[1]
    width = query.shape[2]
    group_count = width // (4 * HD)
    reach = KW // 2
    queries = query[0]
    keys_local = key[0]
    values_local = value[0]
    own_ids = segments[0] + 1
    wide_ids = extended(own_ids, (("seq", 0),), frame_count)
    paired = extended(jnp.stack([keys_local, values_local]), (("seq", 1),), frame_count)

    def forward_group(items):
        return attend(items[0], items[1], items[2], own_ids, wide_ids)

    context_groups, highest, totals = lax.map(
        forward_group, (to_groups(queries), to_groups(paired[0]), to_groups(paired[1]))
    )
    context = from_groups(context_groups)
    context_b = context.astype(jnp.bfloat16)
    attended = jnp.dot(context_b, out_proj, preferred_element_type=jnp.float32).astype(jnp.bfloat16)
    attended_wide = extended(attended, (("seq", 0),), reach)
    conv_ids = wide_ids[frame_count - reach : 2 * frame_count + reach]
    kernel = conv_kernel.astype(jnp.float32)
    masks = [(conv_ids[offset : offset + frame_count] == own_ids)[:, None] for offset in range(KW)]
    convolved = jnp.zeros((frame_count, width), jnp.float32)
    for offset in range(KW):
        convolved = convolved + jnp.where(
            masks[offset],
            kernel[offset] * attended_wide[offset : offset + frame_count].astype(jnp.float32),
            0.0,
        )
    gate = jax.nn.sigmoid(convolved)
    block_out = (convolved * gate).astype(jnp.bfloat16)
    conv_grad = (cotangent[0].astype(jnp.float32) * gate * (1.0 + convolved * (1.0 - gate))).astype(
        jnp.bfloat16
    )
    conv_grad_wide = extended(conv_grad, (("seq", 0),), reach)
    conv_grad_f = conv_grad.astype(jnp.float32)
    attended_grad = jnp.zeros((frame_count, width), jnp.float32)
    kernel_rows = []
    for offset in range(KW):
        mirror = 2 * reach - offset
        attended_grad = attended_grad + jnp.where(
            masks[mirror],
            kernel[offset] * conv_grad_wide[mirror : mirror + frame_count].astype(jnp.float32),
            0.0,
        )
        kernel_rows.append(
            jnp.sum(
                jnp.where(
                    masks[offset],
                    conv_grad_f * attended_wide[offset : offset + frame_count].astype(jnp.float32),
                    0.0,
                ),
                axis=0,
            )
        )
    scale_out = (lax.axis_size("dp") * lax.axis_size("seq") * frame_count) ** (-0.5)
    grad_kernel = lax.psum(jnp.stack(kernel_rows), ("dp", "seq")) * scale_out
    attended_grad_b = attended_grad.astype(jnp.bfloat16)
    reduced = lax.psum_scatter(
        lax.dot_general(
            context_b, attended_grad_b, (((0,), (0,)), ((), ())), preferred_element_type=jnp.float32
        ),
        ("dp", "seq"),
        scatter_dimension=0,
        tiled=True,
    )
    grad_out_proj = reduced * scale_out
    context_grad = lax.dot_general(
        attended_grad_b, out_proj, (((1,), (1,)), ((), ())), preferred_element_type=jnp.float32
    ).astype(jnp.bfloat16)
    products = (to_groups(context_grad).astype(jnp.float32) * to_groups(context)).reshape(
        group_count, frame_count, 4, HD
    )
    deltas = jnp.moveaxis(jnp.sum(products, axis=3), 2, 1)

    def both_group(items):
        probs, score_grad, upstream_heads = score_grads(
            items[0], items[1], items[2], items[3], items[4], items[5], items[6], own_ids, wide_ids
        )
        key_part, value_part = key_side(items[0], items[1], probs, score_grad, upstream_heads)
        return (query_side(items[0], items[1], score_grad), key_part, value_part)

    query_part, key_part, value_part = lax.map(
        both_group,
        (
            to_groups(queries),
            to_groups(paired[0]),
            to_groups(paired[1]),
            to_groups(context_grad),
            highest,
            totals,
            deltas,
        ),
    )
    key_wide = from_groups(key_part)
    value_wide = from_groups(value_part)
    earlier = jnp.stack([key_wide[:frame_count], value_wide[:frame_count]])
    later = jnp.stack([key_wide[2 * frame_count :], value_wide[2 * frame_count :]])
    from_later = from_behind(earlier.astype(jnp.bfloat16), "seq", -1).astype(earlier.dtype)
    from_earlier = from_behind(later.astype(jnp.bfloat16), "seq", 1).astype(later.dtype)
    key_total = key_wide[frame_count : 2 * frame_count] + from_later[0] + from_earlier[0]
    value_total = value_wide[frame_count : 2 * frame_count] + from_later[1] + from_earlier[1]
    grad_query = from_groups(query_part).astype(jnp.bfloat16)
    grad_key = key_total.astype(jnp.bfloat16)
    grad_value = value_total.astype(jnp.bfloat16)
    return (
        block_out[None],
        grad_query[None],
        grad_key[None],
        grad_value[None],
        grad_kernel,
        grad_out_proj,
    )


def solution(mesh):
    in_specs = (
        P("dp", "seq", None),
        P("dp", "seq", None),
        P("dp", "seq", None),
        P("dp", "seq"),
        P(),
        P(),
        P("dp", "seq", None),
    )
    out_specs = (
        P("dp", "seq", None),
        P("dp", "seq", None),
        P("dp", "seq", None),
        P("dp", "seq", None),
        P(),
        P(("dp", "seq"), None),
    )
    return jax.shard_map(
        per_device, mesh=mesh, in_specs=in_specs, out_specs=out_specs, check_vma=False
    )
```

profile of v0, /device:TPU:1, one launch (start us, length us, event | category | flops | bytes accessed | tf_op | source)
XLA Modules:
  0.0 1732.6 jit_solution(641398557045694055)
XLA Ops:
  8.6 15.1 collective-permute-start.1
  23.7 5.0 collective-permute-start.2
  30.7 13.3 collective-permute-start.3
  52.2 2.8 copy.31
  55.0 4.3 copy.33
  59.3 38.1 %while.30 = (s32[]{:T(128)}, f32[6,256,256]{1,2,0:T(8,128)}, f32[6,4,256]{2,1,0:T(4,128)}, f32[6,4,256]{2,1,0:T(4,128)}, bf16[6,768,256]{1,2,0:T(8,128)(2,1)S(1)...) while((s32[]{:T(128)}, f32[6,256,256]{1,2,0:T(8,128)}, ...), condition=%wide.region_3.4_spmd.clone, body=%wide.region_0.3_spmd.sunk.clone | while | flops 210958336 | bytes 13804649 | solution.py:104
  99.8 4.1 convolution_convert_fusion.1
  108.6 3.2 collective-permute-done.5
  112.0 22.7 %fusion.142 = (f32[1536]{0:T(1024)}, f32[1536]{0:T(1024)}, f32[1536]{0:T(1024)}, f32[1536]{0:T(1024)}, f32[1536]{0:T(1024)}, /*index=5*/f32[1536]{0:T(1024)}, bf16[256,1536]{1,0:T(8,128)(2,1)S(1)}, f32[256,1536]{1,0:T(8,128)}) fusion(pred[256]{0:T(512)(128)(4,1)S(1)} %get-tuple-element.289, bf16[15,1536]{1,0:T(8,128)(2,1)S(1)} %collective-permute-done.5, ...), kind=kLoop, calls=%fused_computation.286 | loop fusion | flops 104193024 | bytes 4259328 | tf_op jit(solution)/shard_map/reduce_sum | solution.py:138
  136.7 4.1 collective-permute-start.7
  142.5 24.2 %fusion.149 = bf16[256,1536]{1,0:T(8,128)(2,1)S(1)} fusion(bf16[256,1536]{1,0:T(8,128)(2,1)S(1)} %get-tuple-element.248, bf16[15,1536]{1,0:T(8,128)(2,1)} %collective-permute-done.7, bf16[15,1536]{1,0:T(8,128)(2,1)} %copy-done.74, f32[1536]{0:T(1024)S(1)} %get-tuple-element.174, f32[1536]{0:T(1024)S(1)} %get-tuple-element.175, ...), kind=kLoop, calls=%fused_computation.304 | loop fusion | flops 83755008 | bytes 1863168 | tf_op jit(solution)/shard_map/convert_element_type | solution.py:149
  166.7 5.0 fusion.216
  171.8 723.4 %fusion = f32[8,1536]{1,0:T(8,128)S(1)} fusion(f32[1536,1536]{1,0:T(8,128)} %fusion.216), kind=kCustom, calls=%all-reduce-scatter | all-reduce-scatter fusion | flops 3145729 | bytes 9486336
  897.8 13.3 collective-permute-start.11
  911.0 3.3 collective-permute-start.73
  914.4 3.4 fusion.111
  917.8 13.1 collective-permute-start.12
  930.9 13.1 collective-permute-start.13
  944.0 13.1 collective-permute-start.14
  957.2 13.1 collective-permute-start.15
  970.3 13.1 collective-permute-start.16
  983.5 5.9 fusion.144
  989.4 13.1 collective-permute-start.17
  1002.5 13.1 collective-permute-start.18
  1015.7 13.1 collective-permute-start.19
  1028.8 13.1 collective-permute-start.20
  1042.0 13.1 collective-permute-start.21
  1055.2 3.6 fusion.113
  1058.8 13.1 collective-permute-start.22
  1071.9 13.1 collective-permute-start.23
  1085.0 13.1 collective-permute-start.24
  1098.2 13.1 collective-permute-start.25
  1111.3 13.3 collective-permute-start.26
  1124.7 3.3 fusion.140
  1128.1 13.1 collective-permute-start.27
  1141.2 13.7 collective-permute-start.28
  1154.9 13.1 collective-permute-start.29
  1168.1 13.1 collective-permute-start.30
  1181.2 13.1 collective-permute-start.31
  1194.5 4.6 convolution_convert_fusion
  1200.5 12.7 collective-permute-start.32
  1213.2 13.1 collective-permute-start.33
  1226.4 13.1 collective-permute-start.34
  1239.5 13.1 collective-permute-start.35
  1252.6 13.1 collective-permute-start.36
  1267.5 13.7 collective-permute-start.37
  1281.2 13.1 collective-permute-start.38
  1294.4 13.1 collective-permute-start.39
  1307.5 8.4 collective-permute-start.40
  1318.2 52.4 %while.31 = (s32[]{:T(128)}, bf16[6,256,256]{1,2,0:T(8,128)(2,1)S(1)}, f32[6,768,256]{1,2,0:T(8,128)}, f32[6,768,256]{1,2,0:T(8,128)}, bf16[6,768,256]{1,2,0:T(8...) while((s32[]{:T(128)}, ...), condition=%wide.region_6.7_spmd.clone, body=%wide.region_5.6_spmd.sunk.clone | while | flops 510590976 | bytes 23504016 | solution.py:174
  1370.6 8.6 collective-permute-start.42
  1379.2 3.0 collective-permute-start.43
  1382.3 9.5 collective-permute-start.44
  1391.8 2.9 collective-permute-start.45
  1394.7 8.7 collective-permute-start.46
  1403.4 4.3 bitcast_convert_fusion
  1416.7 4.3 collective-permute-start.52
  1423.8 3.3 collective-permute-start.54
  1432.7 6.0 collective-permute-start.58
  1440.8 4.7 collective-permute-start.60
  1469.0 3.0 collective-permute-start.9
  1485.6 2.9 slice.906
  1489.9 96.9 %concatenate.118 = f32[518,1536]{1,0:T(8,128)} concatenate(f32[6,1536]{1,0:T(8,128)S(1)} %collective-permute-done.73, f32[8,1536]{1,0:T(8,128)} %collective-permute-done.72, f32[8,1536]{1,0:T(8,128)} %collective-permute-done.71, f32[8,1536]{1,0:T(8,128)} %collective-permute-done.70, f32[8,1536]{1,0:T(8,128)} %collective-permute-done.69, f32[8,1536]{1,0:T(8,128)} %collective-permute-done.68, ...), dimensions={0} | concatenate | bytes 6365184
  1588.4 128.7 %all-reduce.4.cloned.1.call-done = f32[31,1536]{1,0:T(8,128)} async-done(((f32[31,1536]{1,0:T(8,128)}), f32[31,1536]{1,0:T(8,128)}) %all-reduce.4.cloned.1.call-update) | async-done | bytes 190480 | tf_op jit(solution)/shard_map/psum | solution.py:148
  (624 shorter events, 185.9 us)
Async XLA Ops:
  7.2 1709.9 %all-reduce.4.cloned.1.call-start = ((), (), s32[]{:S(2)}) async-start(), calls=%async_computation | async-start | bytes 393216 | tf_op jit(solution)/shard_map/psum | solution.py:148
  8.6 39.0 %collective-permute-start.1 = (bf16[2,256,1536]{2,1,0:T(8,128)(2,1)S(1)}, bf16[2,256,1536]{2,1,0:T(8,128)(2,1)}, u32[]{:S(2)}, u32[]{:S(2)}) collective-permute-start(bf16[2,256,1536]{2,1,0:T(8,128)(2,1)S(1)} %constant_dynamic-update-slice_fusion.4), channel_id=1, source_target_pairs={{0,1},{1,2},{2,3},{3,4},{4,5},{5,6},{6,7},{7,8},{8,9},{9,10},{10,1... | collective-permute-start | bytes 4718600 | tf_op jit(solution)/shard_map/ppermute | solution.py:15
  23.7 23.9 %collective-permute-start.2 = (bf16[2,256,1536]{2,1,0:T(8,128)(2,1)S(1)}, bf16[2,256,1536]{2,1,0:T(8,128)(2,1)}, u32[]{:S(2)}, u32[]{:S(2)}) collective-permute-start(bf16[2,256,1536]{2,1,0:T(8,128)(2,1)S(1)} %constant_dynamic-update-slice_fusion.4), channel_id=1, source_target_pairs={{1,0},{2,1},{3,2},{4,3},{5,4},{6,5},{7,6},{8,7},{9,8},{10,9},{11,1... | collective-permute-start | bytes 4718600 | tf_op jit(solution)/shard_map/ppermute | solution.py:18
  28.8 17.0 collective-permute-start
  30.7 16.2 collective-permute-start.3
  895.4 61.8 %collective-permute-start.10 = (f32[8,1536]{1,0:T(8,128)S(1)}, f32[8,1536]{1,0:T(8,128)S(1)}, u32[]{:S(2)}, u32[]{:S(2)}) collective-permute-start(f32[8,1536]{1,0:T(8,128)S(1)} %fusion), channel_id=1, source_target_pairs={{0,1},{1,2},{2,3},{3,4},{4,5},{5,6},{6,7},{7,8},{8,9},{9,10},{10,1... | collective-permute-start | bytes 147464
  897.8 72.5 %collective-permute-start.11 = (f32[8,1536]{1,0:T(8,128)S(1)}, f32[8,1536]{1,0:T(8,128)S(1)}, u32[]{:S(2)}, u32[]{:S(2)}) collective-permute-start(f32[8,1536]{1,0:T(8,128)S(1)} %fusion), channel_id=1, source_target_pairs={{0,2},{1,3},{2,4},{3,5},{4,6},{5,7},{6,8},{7,9},{8,10},{9,11},{10,... | collective-permute-start | bytes 147464
  911.0 33.0 %collective-permute-start.73 = (f32[6,1536]{1,0:T(8,128)S(1)}, f32[6,1536]{1,0:T(8,128)S(1)}, u32[]{:S(2)}, u32[]{:S(2)}) collective-permute-start(f32[6,1536]{1,0:T(8,128)S(1)} %slice.909), channel_id=1, source_target_pairs={{0,64},{1,65},{2,66},{3,67},{4,68},{5,69},{6,70},{7,71},{8,72},{9,... | collective-permute-start | bytes 110600
  917.8 71.6 %collective-permute-start.12 = (f32[8,1536]{1,0:T(8,128)S(1)}, f32[8,1536]{1,0:T(8,128)S(1)}, u32[]{:S(2)}, u32[]{:S(2)}) collective-permute-start(f32[8,1536]{1,0:T(8,128)S(1)} %fusion), channel_id=1, source_target_pairs={{0,3},{1,4},{2,5},{3,6},{4,7},{5,8},{6,9},{7,10},{8,11},{9,12},{10... | collective-permute-start | bytes 147464
  930.9 71.6 %collective-permute-start.13 = (f32[8,1536]{1,0:T(8,128)S(1)}, f32[8,1536]{1,0:T(8,128)S(1)}, u32[]{:S(2)}, u32[]{:S(2)}) collective-permute-start(f32[8,1536]{1,0:T(8,128)S(1)} %fusion), channel_id=1, source_target_pairs={{0,4},{1,5},{2,6},{3,7},{4,8},{5,9},{6,10},{7,11},{8,12},{9,13},{1... | collective-permute-start | bytes 147464
  944.0 71.6 %collective-permute-start.14 = (f32[8,1536]{1,0:T(8,128)S(1)}, f32[8,1536]{1,0:T(8,128)S(1)}, u32[]{:S(2)}, u32[]{:S(2)}) collective-permute-start(f32[8,1536]{1,0:T(8,128)S(1)} %fusion), channel_id=1, source_target_pairs={{0,5},{1,6},{2,7},{3,8},{4,9},{5,10},{6,11},{7,12},{8,13},{9,14},{... | collective-permute-start | bytes 147464
  957.2 71.7 %collective-permute-start.15 = (f32[8,1536]{1,0:T(8,128)S(1)}, f32[8,1536]{1,0:T(8,128)S(1)}, u32[]{:S(2)}, u32[]{:S(2)}) collective-permute-start(f32[8,1536]{1,0:T(8,128)S(1)} %fusion), channel_id=1, source_target_pairs={{0,6},{1,7},{2,8},{3,9},{4,10},{5,11},{6,12},{7,13},{8,14},{9,15},... | collective-permute-start | bytes 147464
  970.3 71.7 %collective-permute-start.16 = (f32[8,1536]{1,0:T(8,128)S(1)}, f32[8,1536]{1,0:T(8,128)S(1)}, u32[]{:S(2)}, u32[]{:S(2)}) collective-permute-start(f32[8,1536]{1,0:T(8,128)S(1)} %fusion), channel_id=1, source_target_pairs={{0,7},{1,8},{2,9},{3,10},{4,11},{5,12},{6,13},{7,14},{8,15},{9,16}... | collective-permute-start | bytes 147464
  989.4 69.4 %collective-permute-start.17 = (f32[8,1536]{1,0:T(8,128)S(1)}, f32[8,1536]{1,0:T(8,128)S(1)}, u32[]{:S(2)}, u32[]{:S(2)}) collective-permute-start(f32[8,1536]{1,0:T(8,128)S(1)} %fusion), channel_id=1, source_target_pairs={{0,8},{1,9},{2,10},{3,11},{4,12},{5,13},{6,14},{7,15},{8,16},{9,17... | collective-permute-start | bytes 147464
  1002.5 69.3 %collective-permute-start.18 = (f32[8,1536]{1,0:T(8,128)S(1)}, f32[8,1536]{1,0:T(8,128)S(1)}, u32[]{:S(2)}, u32[]{:S(2)}) collective-permute-start(f32[8,1536]{1,0:T(8,128)S(1)} %fusion), channel_id=1, source_target_pairs={{0,9},{1,10},{2,11},{3,12},{4,13},{5,14},{6,15},{7,16},{8,17},{9,1... | collective-permute-start | bytes 147464
  1015.7 69.3 %collective-permute-start.19 = (f32[8,1536]{1,0:T(8,128)S(1)}, f32[8,1536]{1,0:T(8,128)S(1)}, u32[]{:S(2)}, u32[]{:S(2)}) collective-permute-start(f32[8,1536]{1,0:T(8,128)S(1)} %fusion), channel_id=1, source_target_pairs={{0,10},{1,11},{2,12},{3,13},{4,14},{5,15},{6,16},{7,17},{8,18},{9,... | collective-permute-start | bytes 147464
  1028.8 69.3 %collective-permute-start.20 = (f32[8,1536]{1,0:T(8,128)S(1)}, f32[8,1536]{1,0:T(8,128)S(1)}, u32[]{:S(2)}, u32[]{:S(2)}) collective-permute-start(f32[8,1536]{1,0:T(8,128)S(1)} %fusion), channel_id=1, source_target_pairs={{0,11},{1,12},{2,13},{3,14},{4,15},{5,16},{6,17},{7,18},{8,19},{9,... | collective-permute-start | bytes 147464
  1042.0 69.3 %collective-permute-start.21 = (f32[8,1536]{1,0:T(8,128)S(1)}, f32[8,1536]{1,0:T(8,128)S(1)}, u32[]{:S(2)}, u32[]{:S(2)}) collective-permute-start(f32[8,1536]{1,0:T(8,128)S(1)} %fusion), channel_id=1, source_target_pairs={{0,12},{1,13},{2,14},{3,15},{4,16},{5,17},{6,18},{7,19},{8,20},{9,... | collective-permute-start | bytes 147464
  1058.8 69.3 %collective-permute-start.22 = (f32[8,1536]{1,0:T(8,128)S(1)}, f32[8,1536]{1,0:T(8,128)S(1)}, u32[]{:S(2)}, u32[]{:S(2)}) collective-permute-start(f32[8,1536]{1,0:T(8,128)S(1)} %fusion), channel_id=1, source_target_pairs={{0,13},{1,14},{2,15},{3,16},{4,17},{5,18},{6,19},{7,20},{8,21},{9,... | collective-permute-start | bytes 147464
  1071.9 69.3 %collective-permute-start.23 = (f32[8,1536]{1,0:T(8,128)S(1)}, f32[8,1536]{1,0:T(8,128)S(1)}, u32[]{:S(2)}, u32[]{:S(2)}) collective-permute-start(f32[8,1536]{1,0:T(8,128)S(1)} %fusion), channel_id=1, source_target_pairs={{0,14},{1,15},{2,16},{3,17},{4,18},{5,19},{6,20},{7,21},{8,22},{9,... | collective-permute-start | bytes 147464
  1085.0 69.9 %collective-permute-start.24 = (f32[8,1536]{1,0:T(8,128)S(1)}, f32[8,1536]{1,0:T(8,128)S(1)}, u32[]{:S(2)}, u32[]{:S(2)}) collective-permute-start(f32[8,1536]{1,0:T(8,128)S(1)} %fusion), channel_id=1, source_target_pairs={{0,15},{1,16},{2,17},{3,18},{4,19},{5,20},{6,21},{7,22},{8,23},{9,... | collective-permute-start | bytes 147464
  1098.2 69.9 %collective-permute-start.25 = (f32[8,1536]{1,0:T(8,128)S(1)}, f32[8,1536]{1,0:T(8,128)S(1)}, u32[]{:S(2)}, u32[]{:S(2)}) collective-permute-start(f32[8,1536]{1,0:T(8,128)S(1)} %fusion), channel_id=1, source_target_pairs={{0,16},{1,17},{2,18},{3,19},{4,20},{5,21},{6,22},{7,23},{8,24},{9,... | collective-permute-start | bytes 147464
  1111.3 69.9 %collective-permute-start.26 = (f32[8,1536]{1,0:T(8,128)S(1)}, f32[8,1536]{1,0:T(8,128)S(1)}, u32[]{:S(2)}, u32[]{:S(2)}) collective-permute-start(f32[8,1536]{1,0:T(8,128)S(1)} %fusion), channel_id=1, source_target_pairs={{0,17},{1,18},{2,19},{3,20},{4,21},{5,22},{6,23},{7,24},{8,25},{9,... | collective-permute-start | bytes 147464
  1128.1 72.5 %collective-permute-start.27 = (f32[8,1536]{1,0:T(8,128)S(1)}, f32[8,1536]{1,0:T(8,128)S(1)}, u32[]{:S(2)}, u32[]{:S(2)}) collective-permute-start(f32[8,1536]{1,0:T(8,128)S(1)} %fusion), channel_id=1, source_target_pairs={{0,18},{1,19},{2,20},{3,21},{4,22},{5,23},{6,24},{7,25},{8,26},{9,... | collective-permute-start | bytes 147464
  1141.2 72.0 %collective-permute-start.28 = (f32[8,1536]{1,0:T(8,128)S(1)}, f32[8,1536]{1,0:T(8,128)}, u32[]{:S(2)}, u32[]{:S(2)}) collective-permute-start(f32[8,1536]{1,0:T(8,128)S(1)} %fusion), channel_id=1, source_target_pairs={{0,19},{1,20},{2,21},{3,22},{4,23},{5,24},{6,25},{7,26},{8,27},{9,... | collective-permute-start | bytes 147464
  1154.9 71.4 %collective-permute-start.29 = (f32[8,1536]{1,0:T(8,128)S(1)}, f32[8,1536]{1,0:T(8,128)}, u32[]{:S(2)}, u32[]{:S(2)}) collective-permute-start(f32[8,1536]{1,0:T(8,128)S(1)} %fusion), channel_id=1, source_target_pairs={{0,20},{1,21},{2,22},{3,23},{4,24},{5,25},{6,26},{7,27},{8,28},{9,... | collective-permute-start | bytes 147464
  1168.1 71.4 %collective-permute-start.30 = (f32[8,1536]{1,0:T(8,128)S(1)}, f32[8,1536]{1,0:T(8,128)}, u32[]{:S(2)}, u32[]{:S(2)}) collective-permute-start(f32[8,1536]{1,0:T(8,128)S(1)} %fusion), channel_id=1, source_target_pairs={{0,21},{1,22},{2,23},{3,24},{4,25},{5,26},{6,27},{7,28},{8,29},{9,... | collective-permute-start | bytes 147464
  1181.2 71.4 %collective-permute-start.31 = (f32[8,1536]{1,0:T(8,128)S(1)}, f32[8,1536]{1,0:T(8,128)}, u32[]{:S(2)}, u32[]{:S(2)}) collective-permute-start(f32[8,1536]{1,0:T(8,128)S(1)} %fusion), channel_id=1, source_target_pairs={{0,22},{1,23},{2,24},{3,25},{4,26},{5,27},{6,28},{7,29},{8,30},{9,... | collective-permute-start | bytes 147464
  1200.5 66.9 %collective-permute-start.32 = (f32[8,1536]{1,0:T(8,128)S(1)}, f32[8,1536]{1,0:T(8,128)S(1)}, u32[]{:S(2)}, u32[]{:S(2)}) collective-permute-start(f32[8,1536]{1,0:T(8,128)S(1)} %fusion), channel_id=1, source_target_pairs={{0,23},{1,24},{2,25},{3,26},{4,27},{5,28},{6,29},{7,30},{8,31},{9,... | collective-permute-start | bytes 147464
  1213.2 68.0 %collective-permute-start.33 = (f32[8,1536]{1,0:T(8,128)S(1)}, f32[8,1536]{1,0:T(8,128)S(1)}, u32[]{:S(2)}, u32[]{:S(2)}) collective-permute-start(f32[8,1536]{1,0:T(8,128)S(1)} %fusion), channel_id=1, source_target_pairs={{0,24},{1,25},{2,26},{3,27},{4,28},{5,29},{6,30},{7,31},{8,32},{9,... | collective-permute-start | bytes 147464
  1226.4 68.0 %collective-permute-start.34 = (f32[8,1536]{1,0:T(8,128)S(1)}, f32[8,1536]{1,0:T(8,128)S(1)}, u32[]{:S(2)}, u32[]{:S(2)}) collective-permute-start(f32[8,1536]{1,0:T(8,128)S(1)} %fusion), channel_id=1, source_target_pairs={{0,25},{1,26},{2,27},{3,28},{4,29},{5,30},{6,31},{7,32},{8,33},{9,... | collective-permute-start | bytes 147464
  1239.5 68.0 %collective-permute-start.35 = (f32[8,1536]{1,0:T(8,128)S(1)}, f32[8,1536]{1,0:T(8,128)S(1)}, u32[]{:S(2)}, u32[]{:S(2)}) collective-permute-start(f32[8,1536]{1,0:T(8,128)S(1)} %fusion), channel_id=1, source_target_pairs={{0,26},{1,27},{2,28},{3,29},{4,30},{5,31},{6,32},{7,33},{8,34},{9,... | collective-permute-start | bytes 147464
  1252.6 63.3 %collective-permute-start.36 = (f32[8,1536]{1,0:T(8,128)S(1)}, f32[8,1536]{1,0:T(8,128)S(1)}, u32[]{:S(2)}, u32[]{:S(2)}) collective-permute-start(f32[8,1536]{1,0:T(8,128)S(1)} %fusion), channel_id=1, source_target_pairs={{0,27},{1,28},{2,29},{3,30},{4,31},{5,32},{6,33},{7,34},{8,35},{9,... | collective-permute-start | bytes 147464
  1267.5 103.1 %collective-permute-start.37 = (f32[8,1536]{1,0:T(8,128)S(1)}, f32[8,1536]{1,0:T(8,128)}, u32[]{:S(2)}, u32[]{:S(2)}) collective-permute-start(f32[8,1536]{1,0:T(8,128)S(1)} %fusion), channel_id=1, source_target_pairs={{0,28},{1,29},{2,30},{3,31},{4,32},{5,33},{6,34},{7,35},{8,36},{9,... | collective-permute-start | bytes 147464
  1281.2 98.0 %collective-permute-start.38 = (f32[8,1536]{1,0:T(8,128)S(1)}, f32[8,1536]{1,0:T(8,128)}, u32[]{:S(2)}, u32[]{:S(2)}) collective-permute-start(f32[8,1536]{1,0:T(8,128)S(1)} %fusion), channel_id=1, source_target_pairs={{0,29},{1,30},{2,31},{3,32},{4,33},{5,34},{6,35},{7,36},{8,37},{9,... | collective-permute-start | bytes 147464
  1294.4 87.9 %collective-permute-start.39 = (f32[8,1536]{1,0:T(8,128)S(1)}, f32[8,1536]{1,0:T(8,128)}, u32[]{:S(2)}, u32[]{:S(2)}) collective-permute-start(f32[8,1536]{1,0:T(8,128)S(1)} %fusion), channel_id=1, source_target_pairs={{0,30},{1,31},{2,32},{3,33},{4,34},{5,35},{6,36},{7,37},{8,38},{9,... | collective-permute-start | bytes 147464
  1307.5 84.3 %collective-permute-start.40 = (f32[8,1536]{1,0:T(8,128)S(1)}, f32[8,1536]{1,0:T(8,128)}, u32[]{:S(2)}, u32[]{:S(2)}) collective-permute-start(f32[8,1536]{1,0:T(8,128)S(1)} %fusion), channel_id=1, source_target_pairs={{0,31},{1,32},{2,33},{3,34},{4,35},{5,36},{6,37},{7,38},{8,39},{9,... | collective-permute-start | bytes 147464
  1315.9 78.8 %collective-permute-start.41 = (f32[8,1536]{1,0:T(8,128)S(1)}, f32[8,1536]{1,0:T(8,128)}, u32[]{:S(2)}, u32[]{:S(2)}) collective-permute-start(f32[8,1536]{1,0:T(8,128)S(1)} %fusion), channel_id=1, source_target_pairs={{0,32},{1,33},{2,34},{3,35},{4,36},{5,37},{6,38},{7,39},{8,40},{9,... | collective-permute-start | bytes 147464
  1370.6 37.2 %collective-permute-start.42 = (f32[8,1536]{1,0:T(8,128)S(1)}, f32[8,1536]{1,0:T(8,128)S(1)}, u32[]{:S(2)}, u32[]{:S(2)}) collective-permute-start(f32[8,1536]{1,0:T(8,128)S(1)} %fusion), channel_id=1, source_target_pairs={{0,33},{1,34},{2,35},{3,36},{4,37},{5,38},{6,39},{7,40},{8,41},{9,... | collective-permute-start | bytes 147464
  1379.2 29.8 %collective-permute-start.43 = (f32[8,1536]{1,0:T(8,128)S(1)}, f32[8,1536]{1,0:T(8,128)S(1)}, u32[]{:S(2)}, u32[]{:S(2)}) collective-permute-start(f32[8,1536]{1,0:T(8,128)S(1)} %fusion), channel_id=1, source_target_pairs={{0,34},{1,35},{2,36},{3,37},{4,38},{5,39},{6,40},{7,41},{8,42},{9,... | collective-permute-start | bytes 147464
  1382.3 29.0 %collective-permute-start.44 = (f32[8,1536]{1,0:T(8,128)S(1)}, f32[8,1536]{1,0:T(8,128)S(1)}, u32[]{:S(2)}, u32[]{:S(2)}) collective-permute-start(f32[8,1536]{1,0:T(8,128)S(1)} %fusion), channel_id=1, source_target_pairs={{0,35},{1,36},{2,37},{3,38},{4,39},{5,40},{6,41},{7,42},{8,43},{9,... | collective-permute-start | bytes 147464
  1391.8 20.9 %collective-permute-start.45 = (f32[8,1536]{1,0:T(8,128)S(1)}, f32[8,1536]{1,0:T(8,128)S(1)}, u32[]{:S(2)}, u32[]{:S(2)}) collective-permute-start(f32[8,1536]{1,0:T(8,128)S(1)} %fusion), channel_id=1, source_target_pairs={{0,36},{1,37},{2,38},{3,39},{4,40},{5,41},{6,42},{7,43},{8,44},{9,... | collective-permute-start | bytes 147464
  1394.7 20.5 %collective-permute-start.46 = (f32[8,1536]{1,0:T(8,128)S(1)}, f32[8,1536]{1,0:T(8,128)S(1)}, u32[]{:S(2)}, u32[]{:S(2)}) collective-permute-start(f32[8,1536]{1,0:T(8,128)S(1)} %fusion), channel_id=1, source_target_pairs={{0,37},{1,38},{2,39},{3,40},{4,41},{5,42},{6,43},{7,44},{8,45},{9,... | collective-permute-start | bytes 147464
  1409.1 12.0 collective-permute-start.48
  1411.3 12.4 collective-permute-start.49
  1412.7 14.3 collective-permute-start.50
  1415.2 13.5 collective-permute-start.51
  1416.7 13.5 collective-permute-start.52
  1423.8 15.0 collective-permute-start.54
  1427.1 13.8 collective-permute-start.55
  1428.7 16.8 collective-permute-start.56
  1430.2 17.9 %collective-permute-start.57 = (f32[8,1536]{1,0:T(8,128)S(1)}, f32[8,1536]{1,0:T(8,128)S(1)}, u32[]{:S(2)}, u32[]{:S(2)}) collective-permute-start(f32[8,1536]{1,0:T(8,128)S(1)} %fusion), channel_id=1, source_target_pairs={{0,48},{1,49},{2,50},{3,51},{4,52},{5,53},{6,54},{7,55},{8,56},{9,... | collective-permute-start | bytes 147464
  1432.7 17.9 %collective-permute-start.58 = (f32[8,1536]{1,0:T(8,128)S(1)}, f32[8,1536]{1,0:T(8,128)S(1)}, u32[]{:S(2)}, u32[]{:S(2)}) collective-permute-start(f32[8,1536]{1,0:T(8,128)S(1)} %fusion), channel_id=1, source_target_pairs={{0,49},{1,50},{2,51},{3,52},{4,53},{5,54},{6,55},{7,56},{8,57},{9,... | collective-permute-start | bytes 147464
  1438.8 13.1 collective-permute-start.59
  1440.8 12.4 collective-permute-start.60
  1451.9 12.6 collective-permute-start.64
  1453.2 13.2 collective-permute-start.65
  1456.0 13.0 collective-permute-start.66
  1460.2 16.6 collective-permute-start.67
  1462.6 16.2 collective-permute-start.68
  1464.5 16.2 collective-permute-start.69
  1466.4 252.4 %collective-permute-start.8 = (bf16[2,256,1536]{1,2,0:T(8,128)(2,1)}, bf16[2,256,1536]{1,2,0:T(8,128)(2,1)}, u32[]{:S(2)}, u32[]{:S(2)}) collective-permute-start(bf16[2,256,1536]{1,2,0:T(8,128)(2,1)} %pad_maximum_fusion.1), channel_id=1, source_target_pairs={{1,0},{2,1},{3,2},{4,3},{5,4},{6,5},{7,6},{8,7},{9,8},{10,9},{11,1... | collective-permute-start | bytes 4718600 | tf_op jit(solution)/shard_map/ppermute | solution.py:26
  1469.0 251.5 %collective-permute-start.9 = (bf16[2,256,1536]{1,2,0:T(8,128)(2,1)}, bf16[2,256,1536]{1,2,0:T(8,128)(2,1)}, u32[]{:S(2)}, u32[]{:S(2)}) collective-permute-start(bf16[2,256,1536]{1,2,0:T(8,128)(2,1)} %pad_maximum_fusion.2), channel_id=1, source_target_pairs={{0,1},{1,2},{2,3},{3,4},{4,5},{5,6},{6,7},{7,8},{8,9},{9,10},{10,1... | collective-permute-start | bytes 4718600 | tf_op jit(solution)/shard_map/ppermute | solution.py:26
  1476.8 12.9 collective-permute-start.70
  (169 other events, 9938.3 us)
Sparse Core Ops, SparseCore 0:
  1476.9 240.1 all-reduce.3
where the time goes:
time: 1750 us; the launch traced here: 1730 us
  blocking collectives  723 us (41%)
  starting transfers between devices  543 us (31%)
  local copies, waits for them, and re-layouts  176 us (10%)
  waiting for transfers between devices  133 us (8%)
  other arithmetic  95.4 us (5%)
  matrix products  43.9 us (3%)
  between operations  17.7 us (1%)
    unnamed x1, blocking collectives  723 us
    unnamed x64, starting transfers between devices  491 us
    psum x1, waiting for transfers between devices, per_device(): grad_kernel = lax.psum(jnp.stack(kernel_rows), ('dp', 'seq')) * scale_out  129 us
    unnamed x323, local copies, waits for them, and re-layouts  104 us
    reduce_sum x6, other arithmetic, per_device(): jnp.sum(jnp.where(masks[offset], conv_grad_f * attended_wide[offset:offse...  40.2 us
  transfers between devices with their start and end apart: 75, of which 3 were waited for; matrix products, arithmetic and copies ran while one was open for 11% of the time, Pallas kernels for 0%

commit v1 on v0

--- a/solution.py
+++ b/solution.py
@@ -145,7 +145,7 @@
             )
         )
     scale_out = (lax.axis_size("dp") * lax.axis_size("seq") * frame_count) ** (-0.5)
-    grad_kernel = lax.psum(jnp.stack(kernel_rows), ("dp", "seq")) * scale_out
+    grad_kernel = jnp.sum(lax.all_gather(jnp.stack(kernel_rows), ("dp", "seq")), axis=0) * scale_out
     attended_grad_b = attended_grad.astype(jnp.bfloat16)
     reduced = lax.psum_scatter(
         lax.dot_general(

time: 1750 us -> 1680 us (0.960)
  waiting for transfers between devices: 133 us -> 3.79 us
  starting transfers between devices: 543 us -> 571 us
    psum x1 -> x0, waiting for transfers between devices: 129 us -> none  [per_device(): grad_kernel = lax.psum(jnp.stack(kernel_rows), ('dp', 'seq')) * scale_out]
    unnamed x64, starting transfers between devices: 491 us -> 518 us
    reduce_sum x0 -> x1, other arithmetic: none -> 17.7 us  [per_device(): jnp.sum(lax.all_gather(jnp.stack(kernel_rows), ('dp', 'seq')), axis=0)]
    unnamed x323 -> x205, local copies, waits for them, and re-layouts: 104 us -> 105 us
  transfers between devices with their start and end apart: 75 -> 75, of which waited for: 3 -> 3; matrix products, arithmetic and copies ran while one was open for 11% -> 57% of each run, Pallas kernels for 0% -> 0%
where the time goes in v1:
time: 1680 us; the launch traced here: 1660 us
  blocking collectives  738 us (44%)
  starting transfers between devices  571 us (34%)
  local copies, waits for them, and re-layouts  183 us (11%)
  other arithmetic  108 us (6%)
  matrix products  43.8 us (3%)
  between operations  17.1 us (1%)
    unnamed x1, blocking collectives  738 us
    unnamed x64, starting transfers between devices  518 us
    unnamed x205, local copies, waits for them, and re-layouts  105 us
    reduce_sum x6, other arithmetic, per_device(): jnp.sum(jnp.where(masks[offset], conv_grad_f * attended_wide[offset:offse...  37.2 us
  transfers between devices with their start and end apart: 75, of which 3 were waited for; matrix products, arithmetic and copies ran while one was open for 57% of the time, Pallas kernels for 0%

profile of v1, /device:TPU:1, one launch (start us, length us, event | category | flops | bytes accessed | tf_op | source)
XLA Modules:
  0.0 1664.8 jit_solution(14681811792974345620)
XLA Ops:
  8.6 5.2 collective-permute-start.2
  13.8 11.9 collective-permute-start.1
  25.7 3.5 collective-permute-start
  29.3 12.4 collective-permute-start.3
  52.1 4.3 copy.33
  56.4 32.8 %while.30 = (s32[]{:T(128)}, f32[6,256,256]{1,2,0:T(8,128)}, f32[6,4,256]{2,1,0:T(4,128)}, f32[6,4,256]{2,1,0:T(4,128)}, bf16[6,768,256]{1,2,0:T(8,128)(2,1)S(1)...) while((s32[]{:T(128)}, f32[6,256,256]{1,2,0:T(8,128)}, ...), condition=%wide.region_3.4_spmd.clone, body=%wide.region_0.3_spmd.sunk.clone | while | flops 210958336 | bytes 13803641 | solution.py:104
  91.0 4.0 convolution_convert_fusion.1
  97.5 3.4 collective-permute-start.4
  101.9 22.1 %fusion.142 = (f32[1536]{0:T(1024)S(1)}, f32[1536]{0:T(1024)S(1)}, f32[1536]{0:T(1024)S(1)}, f32[1536]{0:T(1024)S(1)}, f32[1536]{0:T(1024)S(1)}, /*index=5*/f32[...) fusion(pred[256]{0:T(512)(128)(4,1)S(1)} %get-tuple-element.289, ...), kind=kLoop, calls=%fused_computation.286 | loop fusion | flops 104193024 | bytes 4259328 | tf_op jit(solution)/shard_map/reduce_sum | solution.py:138
  128.3 3.0 fusion.113
  134.4 5.3 fusion.144
  147.5 4.3 stack.161
  151.8 4.3 collective-permute-start.7
  161.6 23.9 %fusion.149 = bf16[256,1536]{1,0:T(8,128)(2,1)S(1)} fusion(bf16[256,1536]{1,0:T(8,128)(2,1)S(1)} %get-tuple-element.248, bf16[15,1536]{1,0:T(8,128)(2,1)} %collective-permute-done.7, bf16[15,1536]{1,0:T(8,128)(2,1)} %collective-permute-done.6, f32[1536]{0:T(1024)S(1)} %get-tuple-element.174, f32[1536]{0:T(1024)S(1)} %get-tuple-element.175, ...), kind=kLoop, calls=%fused_computation.304 | loop fusion | flops 83755008 | bytes 1863168 | tf_op jit(solution)/shard_map/convert_element_type | solution.py:149
  186.4 5.0 fusion.216
  191.4 737.7 %fusion = f32[8,1536]{1,0:T(8,128)S(1)} fusion(f32[1536,1536]{1,0:T(8,128)} %fusion.216), kind=kCustom, calls=%all-reduce-scatter | all-reduce-scatter fusion | flops 3145729 | bytes 9486336
  934.3 4.6 convolution_convert_fusion
  943.5 55.6 %while.31 = (s32[]{:T(128)}, bf16[6,256,256]{1,2,0:T(8,128)(2,1)}, f32[6,768,256]{1,2,0:T(8,128)}, f32[6,768,256]{1,2,0:T(8,128)}, bf16[6,768,256]{1,2,0:T(8,128...) while((s32[]{:T(128)}, bf16[6,256,256]{1,2,0:T(8,128)(2,1)}, ...), condition=%wide.region_6.7_spmd.clone, body=%wide.region_5.6_spmd.sunk.clone | while | flops 510590976 | bytes 23503008 | solution.py:174
  999.1 4.2 bitcast_convert_fusion
  1018.8 5.3 collective-permute-start.8
  1026.7 13.1 collective-permute-start.58
  1039.8 5.3 collective-permute-start.57
  1045.1 23.1 %collective-permute-start.56 = (f32[8,1536]{1,0:T(8,128)S(1)}, f32[8,1536]{1,0:T(8,128)S(1)}, u32[]{:S(2)}, u32[]{:S(2)}) collective-permute-start(f32[8,1536]{1,0:T(8,128)S(1)} %fusion), channel_id=1, source_target_pairs={{0,47},{1,48},{2,49},{3,50},{4,51},{5,52},{6,53},{7,54},{8,55},{9,... | collective-permute-start | bytes 147464
  1069.6 12.1 collective-permute-start.54
  1086.0 5.8 collective-permute-start.51
  1093.1 7.6 collective-permute-start.49
  1102.1 5.4 collective-permute-start.47
  1110.3 3.2 collective-permute-start.45
  1113.6 6.9 collective-permute-start.44
  1120.6 4.6 collective-permute-start.43
  1125.2 5.5 collective-permute-start.42
  1132.3 3.6 collective-permute-start.40
  1135.9 8.9 collective-permute-start.39
  1144.8 13.1 collective-permute-start.38
  1158.0 13.1 collective-permute-start.37
  1171.1 13.1 collective-permute-start.36
  1184.3 13.1 collective-permute-start.35
  1197.4 13.1 collective-permute-start.34
  1210.6 13.1 collective-permute-start.33
  1223.7 13.1 collective-permute-start.32
  1236.9 13.1 collective-permute-start.31
  1250.0 13.1 collective-permute-start.30
  1263.2 13.1 collective-permute-start.29
  1276.3 13.1 collective-permute-start.28
  1289.5 13.1 collective-permute-start.27
  1302.6 13.1 collective-permute-start.26
  1315.8 13.1 collective-permute-start.25
  1328.9 13.1 collective-permute-start.24
  1342.1 13.1 collective-permute-start.23
  1355.2 13.1 collective-permute-start.22
  1368.4 13.1 collective-permute-start.21
  1381.5 13.1 collective-permute-start.20
  1394.7 13.1 collective-permute-start.19
  1407.8 13.1 collective-permute-start.18
  1421.0 13.1 collective-permute-start.17
  1434.1 13.1 collective-permute-start.16
  1447.3 13.7 collective-permute-start.15
  1461.0 13.1 collective-permute-start.14
  1474.2 13.2 collective-permute-start.13
  1487.7 13.2 collective-permute-start.12
  1500.8 13.1 collective-permute-start.11
  1514.0 12.7 collective-permute-start.10
  1534.0 97.0 %concatenate.118 = f32[518,1536]{1,0:T(8,128)} concatenate(f32[6,1536]{1,0:T(8,128)S(1)} %collective-permute-done.73, f32[8,1536]{1,0:T(8,128)S(1)} %collective-permute-done.72, f32[8,1536]{1,0:T(8,128)S(1)} %collective-permute-done.71, f32[8,1536]{1,0:T(8,128)S(1)} %collective-permute-done.70, f32[8,1536]{1,0:T(8,128)S(1)} %collective-permute-done.69, ...), dimensions={0} | concatenate | bytes 6365184
  1639.4 17.7 %reduce_sum.338 = f32[31,1536]{1,0:T(8,128)S(1)} reduce(f32[256,31,1536]{2,1,0:T(8,128)} %all-gather.4.cloned.1.call-done, f32[]{:T(128)} %constant.56.clone.1), dimensions={0}, to_apply=%region_38.39 | reduce | flops 12142080 | bytes 48949252 | tf_op jit(solution)/shard_map/reduce_sum | solution.py:148
  (507 shorter events, 182.1 us)
Async XLA Ops:
  7.2 1632.2 %all-gather.4.cloned.1.call-start = ((), (), s32[]{:S(2)}) async-start(), calls=%async_computation | async-start | bytes 50528256 | tf_op jit(solution)/shard_map/all_gather | solution.py:148
  8.6 36.2 %collective-permute-start.2 = (bf16[2,256,1536]{2,1,0:T(8,128)(2,1)S(1)}, bf16[2,256,1536]{2,1,0:T(8,128)(2,1)}, u32[]{:S(2)}, u32[]{:S(2)}) collective-permute-start(bf16[2,256,1536]{2,1,0:T(8,128)(2,1)S(1)} %constant_dynamic-update-slice_fusion.4), channel_id=1, source_target_pairs={{1,0},{2,1},{3,2},{4,3},{5,4},{6,5},{7,6},{8,7},{9,8},{10,9},{11,1... | collective-permute-start | bytes 4718600 | tf_op jit(solution)/shard_map/ppermute | solution.py:18
  13.8 31.1 %collective-permute-start.1 = (bf16[2,256,1536]{2,1,0:T(8,128)(2,1)S(1)}, bf16[2,256,1536]{2,1,0:T(8,128)(2,1)}, u32[]{:S(2)}, u32[]{:S(2)}) collective-permute-start(bf16[2,256,1536]{2,1,0:T(8,128)(2,1)S(1)} %constant_dynamic-update-slice_fusion.4), channel_id=1, source_target_pairs={{0,1},{1,2},{2,3},{3,4},{4,5},{5,6},{6,7},{7,8},{8,9},{9,10},{10,1... | collective-permute-start | bytes 4718600 | tf_op jit(solution)/shard_map/ppermute | solution.py:15
  25.7 17.9 %collective-permute-start = (s32[256]{0:T(256)S(1)}, s32[256]{0:T(256)S(1)}, u32[]{:S(2)}, u32[]{:S(2)}) collective-permute-start(s32[256]{0:T(256)S(1)} %bitcast.195), channel_id=1, source_target_pairs={{0,1},{1,2},{2,3},{3,4},{4,5},{5,6},{6,7},{7,8},{8,9},{9,10},{10,1... | collective-permute-start | bytes 3080 | tf_op jit(solution)/shard_map/ppermute | solution.py:15
  29.3 15.3 collective-permute-start.3
  929.1 75.8 %collective-permute-start.72 = (f32[8,1536]{1,0:T(8,128)S(1)}, f32[8,1536]{1,0:T(8,128)S(1)}, u32[]{:S(2)}, u32[]{:S(2)}) collective-permute-start(f32[8,1536]{1,0:T(8,128)S(1)} %fusion), channel_id=1, source_target_pairs={{0,63},{1,64},{2,65},{3,66},{4,67},{5,68},{6,69},{7,70},{8,71},{9,... | collective-permute-start | bytes 147464
  930.4 75.8 %collective-permute-start.71 = (f32[8,1536]{1,0:T(8,128)S(1)}, f32[8,1536]{1,0:T(8,128)S(1)}, u32[]{:S(2)}, u32[]{:S(2)}) collective-permute-start(f32[8,1536]{1,0:T(8,128)S(1)} %fusion), channel_id=1, source_target_pairs={{0,62},{1,63},{2,64},{3,65},{4,66},{5,67},{6,68},{7,69},{8,70},{9,... | collective-permute-start | bytes 147464
  931.7 77.2 %collective-permute-start.70 = (f32[8,1536]{1,0:T(8,128)S(1)}, f32[8,1536]{1,0:T(8,128)S(1)}, u32[]{:S(2)}, u32[]{:S(2)}) collective-permute-start(f32[8,1536]{1,0:T(8,128)S(1)} %fusion), channel_id=1, source_target_pairs={{0,61},{1,62},{2,63},{3,64},{4,65},{5,66},{6,67},{7,68},{8,69},{9,... | collective-permute-start | bytes 147464
  933.0 77.2 %collective-permute-start.69 = (f32[8,1536]{1,0:T(8,128)S(1)}, f32[8,1536]{1,0:T(8,128)S(1)}, u32[]{:S(2)}, u32[]{:S(2)}) collective-permute-start(f32[8,1536]{1,0:T(8,128)S(1)} %fusion), channel_id=1, source_target_pairs={{0,60},{1,61},{2,62},{3,63},{4,64},{5,65},{6,66},{7,67},{8,68},{9,... | collective-permute-start | bytes 147464
  940.4 63.3 %collective-permute-start.73 = (f32[6,1536]{1,0:T(8,128)S(1)}, f32[6,1536]{1,0:T(8,128)S(1)}, u32[]{:S(2)}, u32[]{:S(2)}) collective-permute-start(f32[6,1536]{1,0:T(8,128)S(1)} %slice.909), channel_id=1, source_target_pairs={{0,64},{1,65},{2,66},{3,67},{4,68},{5,69},{6,70},{7,71},{8,72},{9,... | collective-permute-start | bytes 110600
  1011.5 12.6 collective-permute-start.63
  1012.8 12.6 collective-permute-start.62
  1014.1 12.6 collective-permute-start.61
  1016.7 615.9 %collective-permute-start.9 = (bf16[2,256,1536]{1,2,0:T(8,128)(2,1)}, bf16[2,256,1536]{1,2,0:T(8,128)(2,1)}, u32[]{:S(2)}, u32[]{:S(2)}) collective-permute-start(bf16[2,256,1536]{1,2,0:T(8,128)(2,1)} %pad_maximum_fusion.2), channel_id=1, source_target_pairs={{0,1},{1,2},{2,3},{3,4},{4,5},{5,6},{6,7},{7,8},{8,9},{9,10},{10,1... | collective-permute-start | bytes 4718600 | tf_op jit(solution)/shard_map/ppermute | solution.py:26
  1018.8 615.5 %collective-permute-start.8 = (bf16[2,256,1536]{1,2,0:T(8,128)(2,1)}, bf16[2,256,1536]{1,2,0:T(8,128)(2,1)}, u32[]{:S(2)}, u32[]{:S(2)}) collective-permute-start(bf16[2,256,1536]{1,2,0:T(8,128)(2,1)} %pad_maximum_fusion.1), channel_id=1, source_target_pairs={{1,0},{2,1},{3,2},{4,3},{5,4},{6,5},{7,6},{8,7},{9,8},{10,9},{11,1... | collective-permute-start | bytes 4718600 | tf_op jit(solution)/shard_map/ppermute | solution.py:26
  1024.1 15.7 collective-permute-start.60
  1025.4 19.7 %collective-permute-start.59 = (f32[8,1536]{1,0:T(8,128)S(1)}, f32[8,1536]{1,0:T(8,128)S(1)}, u32[]{:S(2)}, u32[]{:S(2)}) collective-permute-start(f32[8,1536]{1,0:T(8,128)S(1)} %fusion), channel_id=1, source_target_pairs={{0,50},{1,51},{2,52},{3,53},{4,54},{5,55},{6,56},{7,57},{8,58},{9,... | collective-permute-start | bytes 147464
  1026.7 41.5 %collective-permute-start.58 = (f32[8,1536]{1,0:T(8,128)S(1)}, f32[8,1536]{1,0:T(8,128)S(1)}, u32[]{:S(2)}, u32[]{:S(2)}) collective-permute-start(f32[8,1536]{1,0:T(8,128)S(1)} %fusion), channel_id=1, source_target_pairs={{0,49},{1,50},{2,51},{3,52},{4,53},{5,54},{6,55},{7,56},{8,57},{9,... | collective-permute-start | bytes 147464
  1039.8 29.7 %collective-permute-start.57 = (f32[8,1536]{1,0:T(8,128)S(1)}, f32[8,1536]{1,0:T(8,128)S(1)}, u32[]{:S(2)}, u32[]{:S(2)}) collective-permute-start(f32[8,1536]{1,0:T(8,128)S(1)} %fusion), channel_id=1, source_target_pairs={{0,48},{1,49},{2,50},{3,51},{4,52},{5,53},{6,54},{7,55},{8,56},{9,... | collective-permute-start | bytes 147464
  1045.1 36.5 %collective-permute-start.56 = (f32[8,1536]{1,0:T(8,128)S(1)}, f32[8,1536]{1,0:T(8,128)S(1)}, u32[]{:S(2)}, u32[]{:S(2)}) collective-permute-start(f32[8,1536]{1,0:T(8,128)S(1)} %fusion), channel_id=1, source_target_pairs={{0,47},{1,48},{2,49},{3,50},{4,51},{5,52},{6,53},{7,54},{8,55},{9,... | collective-permute-start | bytes 147464
  1068.2 14.8 collective-permute-start.55
  1069.6 16.4 collective-permute-start.54
  1081.7 10.1 collective-permute-start.53
  1086.0 14.8 collective-permute-start.51
  1091.8 10.3 collective-permute-start.50
  1093.1 14.4 collective-permute-start.49
  1102.1 11.5 collective-permute-start.47
  1107.5 13.0 collective-permute-start.46
  1110.3 14.8 collective-permute-start.45
  1113.6 17.0 %collective-permute-start.44 = (f32[8,1536]{1,0:T(8,128)S(1)}, f32[8,1536]{1,0:T(8,128)S(1)}, u32[]{:S(2)}, u32[]{:S(2)}) collective-permute-start(f32[8,1536]{1,0:T(8,128)S(1)} %fusion), channel_id=1, source_target_pairs={{0,35},{1,36},{2,37},{3,38},{4,39},{5,40},{6,41},{7,42},{8,43},{9,... | collective-permute-start | bytes 147464
  1120.6 11.7 collective-permute-start.43
  1125.2 10.7 collective-permute-start.42
  1130.7 14.1 collective-permute-start.41
  1132.3 25.7 %collective-permute-start.40 = (f32[8,1536]{1,0:T(8,128)S(1)}, f32[8,1536]{1,0:T(8,128)S(1)}, u32[]{:S(2)}, u32[]{:S(2)}) collective-permute-start(f32[8,1536]{1,0:T(8,128)S(1)} %fusion), channel_id=1, source_target_pairs={{0,31},{1,32},{2,33},{3,34},{4,35},{5,36},{6,37},{7,38},{8,39},{9,... | collective-permute-start | bytes 147464
  1135.9 35.2 %collective-permute-start.39 = (f32[8,1536]{1,0:T(8,128)S(1)}, f32[8,1536]{1,0:T(8,128)S(1)}, u32[]{:S(2)}, u32[]{:S(2)}) collective-permute-start(f32[8,1536]{1,0:T(8,128)S(1)} %fusion), channel_id=1, source_target_pairs={{0,30},{1,31},{2,32},{3,33},{4,34},{5,35},{6,36},{7,37},{8,38},{9,... | collective-permute-start | bytes 147464
  1144.8 39.4 %collective-permute-start.38 = (f32[8,1536]{1,0:T(8,128)S(1)}, f32[8,1536]{1,0:T(8,128)S(1)}, u32[]{:S(2)}, u32[]{:S(2)}) collective-permute-start(f32[8,1536]{1,0:T(8,128)S(1)} %fusion), channel_id=1, source_target_pairs={{0,29},{1,30},{2,31},{3,32},{4,33},{5,34},{6,35},{7,36},{8,37},{9,... | collective-permute-start | bytes 147464
  1158.0 39.4 %collective-permute-start.37 = (f32[8,1536]{1,0:T(8,128)S(1)}, f32[8,1536]{1,0:T(8,128)S(1)}, u32[]{:S(2)}, u32[]{:S(2)}) collective-permute-start(f32[8,1536]{1,0:T(8,128)S(1)} %fusion), channel_id=1, source_target_pairs={{0,28},{1,29},{2,30},{3,31},{4,32},{5,33},{6,34},{7,35},{8,36},{9,... | collective-permute-start | bytes 147464
  1171.1 39.4 %collective-permute-start.36 = (f32[8,1536]{1,0:T(8,128)S(1)}, f32[8,1536]{1,0:T(8,128)S(1)}, u32[]{:S(2)}, u32[]{:S(2)}) collective-permute-start(f32[8,1536]{1,0:T(8,128)S(1)} %fusion), channel_id=1, source_target_pairs={{0,27},{1,28},{2,29},{3,30},{4,31},{5,32},{6,33},{7,34},{8,35},{9,... | collective-permute-start | bytes 147464
  1184.3 39.4 %collective-permute-start.35 = (f32[8,1536]{1,0:T(8,128)S(1)}, f32[8,1536]{1,0:T(8,128)S(1)}, u32[]{:S(2)}, u32[]{:S(2)}) collective-permute-start(f32[8,1536]{1,0:T(8,128)S(1)} %fusion), channel_id=1, source_target_pairs={{0,26},{1,27},{2,28},{3,29},{4,30},{5,31},{6,32},{7,33},{8,34},{9,... | collective-permute-start | bytes 147464
  1197.4 39.4 %collective-permute-start.34 = (f32[8,1536]{1,0:T(8,128)S(1)}, f32[8,1536]{1,0:T(8,128)S(1)}, u32[]{:S(2)}, u32[]{:S(2)}) collective-permute-start(f32[8,1536]{1,0:T(8,128)S(1)} %fusion), channel_id=1, source_target_pairs={{0,25},{1,26},{2,27},{3,28},{4,29},{5,30},{6,31},{7,32},{8,33},{9,... | collective-permute-start | bytes 147464
  1210.6 39.4 %collective-permute-start.33 = (f32[8,1536]{1,0:T(8,128)S(1)}, f32[8,1536]{1,0:T(8,128)S(1)}, u32[]{:S(2)}, u32[]{:S(2)}) collective-permute-start(f32[8,1536]{1,0:T(8,128)S(1)} %fusion), channel_id=1, source_target_pairs={{0,24},{1,25},{2,26},{3,27},{4,28},{5,29},{6,30},{7,31},{8,32},{9,... | collective-permute-start | bytes 147464
  1223.7 39.4 %collective-permute-start.32 = (f32[8,1536]{1,0:T(8,128)S(1)}, f32[8,1536]{1,0:T(8,128)S(1)}, u32[]{:S(2)}, u32[]{:S(2)}) collective-permute-start(f32[8,1536]{1,0:T(8,128)S(1)} %fusion), channel_id=1, source_target_pairs={{0,23},{1,24},{2,25},{3,26},{4,27},{5,28},{6,29},{7,30},{8,31},{9,... | collective-permute-start | bytes 147464
  1236.9 39.4 %collective-permute-start.31 = (f32[8,1536]{1,0:T(8,128)S(1)}, f32[8,1536]{1,0:T(8,128)S(1)}, u32[]{:S(2)}, u32[]{:S(2)}) collective-permute-start(f32[8,1536]{1,0:T(8,128)S(1)} %fusion), channel_id=1, source_target_pairs={{0,22},{1,23},{2,24},{3,25},{4,26},{5,27},{6,28},{7,29},{8,30},{9,... | collective-permute-start | bytes 147464
  1250.0 39.4 %collective-permute-start.30 = (f32[8,1536]{1,0:T(8,128)S(1)}, f32[8,1536]{1,0:T(8,128)S(1)}, u32[]{:S(2)}, u32[]{:S(2)}) collective-permute-start(f32[8,1536]{1,0:T(8,128)S(1)} %fusion), channel_id=1, source_target_pairs={{0,21},{1,22},{2,23},{3,24},{4,25},{5,26},{6,27},{7,28},{8,29},{9,... | collective-permute-start | bytes 147464
  1263.2 39.4 %collective-permute-start.29 = (f32[8,1536]{1,0:T(8,128)S(1)}, f32[8,1536]{1,0:T(8,128)S(1)}, u32[]{:S(2)}, u32[]{:S(2)}) collective-permute-start(f32[8,1536]{1,0:T(8,128)S(1)} %fusion), channel_id=1, source_target_pairs={{0,20},{1,21},{2,22},{3,23},{4,24},{5,25},{6,26},{7,27},{8,28},{9,... | collective-permute-start | bytes 147464
  1276.3 39.4 %collective-permute-start.28 = (f32[8,1536]{1,0:T(8,128)S(1)}, f32[8,1536]{1,0:T(8,128)S(1)}, u32[]{:S(2)}, u32[]{:S(2)}) collective-permute-start(f32[8,1536]{1,0:T(8,128)S(1)} %fusion), channel_id=1, source_target_pairs={{0,19},{1,20},{2,21},{3,22},{4,23},{5,24},{6,25},{7,26},{8,27},{9,... | collective-permute-start | bytes 147464
  1289.5 39.4 %collective-permute-start.27 = (f32[8,1536]{1,0:T(8,128)S(1)}, f32[8,1536]{1,0:T(8,128)S(1)}, u32[]{:S(2)}, u32[]{:S(2)}) collective-permute-start(f32[8,1536]{1,0:T(8,128)S(1)} %fusion), channel_id=1, source_target_pairs={{0,18},{1,19},{2,20},{3,21},{4,22},{5,23},{6,24},{7,25},{8,26},{9,... | collective-permute-start | bytes 147464
  1302.6 39.4 %collective-permute-start.26 = (f32[8,1536]{1,0:T(8,128)S(1)}, f32[8,1536]{1,0:T(8,128)S(1)}, u32[]{:S(2)}, u32[]{:S(2)}) collective-permute-start(f32[8,1536]{1,0:T(8,128)S(1)} %fusion), channel_id=1, source_target_pairs={{0,17},{1,18},{2,19},{3,20},{4,21},{5,22},{6,23},{7,24},{8,25},{9,... | collective-permute-start | bytes 147464
  1315.8 39.4 %collective-permute-start.25 = (f32[8,1536]{1,0:T(8,128)S(1)}, f32[8,1536]{1,0:T(8,128)S(1)}, u32[]{:S(2)}, u32[]{:S(2)}) collective-permute-start(f32[8,1536]{1,0:T(8,128)S(1)} %fusion), channel_id=1, source_target_pairs={{0,16},{1,17},{2,18},{3,19},{4,20},{5,21},{6,22},{7,23},{8,24},{9,... | collective-permute-start | bytes 147464
  1328.9 39.4 %collective-permute-start.24 = (f32[8,1536]{1,0:T(8,128)S(1)}, f32[8,1536]{1,0:T(8,128)S(1)}, u32[]{:S(2)}, u32[]{:S(2)}) collective-permute-start(f32[8,1536]{1,0:T(8,128)S(1)} %fusion), channel_id=1, source_target_pairs={{0,15},{1,16},{2,17},{3,18},{4,19},{5,20},{6,21},{7,22},{8,23},{9,... | collective-permute-start | bytes 147464
  1342.1 39.4 %collective-permute-start.23 = (f32[8,1536]{1,0:T(8,128)S(1)}, f32[8,1536]{1,0:T(8,128)S(1)}, u32[]{:S(2)}, u32[]{:S(2)}) collective-permute-start(f32[8,1536]{1,0:T(8,128)S(1)} %fusion), channel_id=1, source_target_pairs={{0,14},{1,15},{2,16},{3,17},{4,18},{5,19},{6,20},{7,21},{8,22},{9,... | collective-permute-start | bytes 147464
  1355.2 39.4 %collective-permute-start.22 = (f32[8,1536]{1,0:T(8,128)S(1)}, f32[8,1536]{1,0:T(8,128)S(1)}, u32[]{:S(2)}, u32[]{:S(2)}) collective-permute-start(f32[8,1536]{1,0:T(8,128)S(1)} %fusion), channel_id=1, source_target_pairs={{0,13},{1,14},{2,15},{3,16},{4,17},{5,18},{6,19},{7,20},{8,21},{9,... | collective-permute-start | bytes 147464
  1368.4 39.4 %collective-permute-start.21 = (f32[8,1536]{1,0:T(8,128)S(1)}, f32[8,1536]{1,0:T(8,128)S(1)}, u32[]{:S(2)}, u32[]{:S(2)}) collective-permute-start(f32[8,1536]{1,0:T(8,128)S(1)} %fusion), channel_id=1, source_target_pairs={{0,12},{1,13},{2,14},{3,15},{4,16},{5,17},{6,18},{7,19},{8,20},{9,... | collective-permute-start | bytes 147464
  1381.5 39.4 %collective-permute-start.20 = (f32[8,1536]{1,0:T(8,128)S(1)}, f32[8,1536]{1,0:T(8,128)S(1)}, u32[]{:S(2)}, u32[]{:S(2)}) collective-permute-start(f32[8,1536]{1,0:T(8,128)S(1)} %fusion), channel_id=1, source_target_pairs={{0,11},{1,12},{2,13},{3,14},{4,15},{5,16},{6,17},{7,18},{8,19},{9,... | collective-permute-start | bytes 147464
  1394.7 39.4 %collective-permute-start.19 = (f32[8,1536]{1,0:T(8,128)S(1)}, f32[8,1536]{1,0:T(8,128)S(1)}, u32[]{:S(2)}, u32[]{:S(2)}) collective-permute-start(f32[8,1536]{1,0:T(8,128)S(1)} %fusion), channel_id=1, source_target_pairs={{0,10},{1,11},{2,12},{3,13},{4,14},{5,15},{6,16},{7,17},{8,18},{9,... | collective-permute-start | bytes 147464
  1407.8 39.4 %collective-permute-start.18 = (f32[8,1536]{1,0:T(8,128)S(1)}, f32[8,1536]{1,0:T(8,128)S(1)}, u32[]{:S(2)}, u32[]{:S(2)}) collective-permute-start(f32[8,1536]{1,0:T(8,128)S(1)} %fusion), channel_id=1, source_target_pairs={{0,9},{1,10},{2,11},{3,12},{4,13},{5,14},{6,15},{7,16},{8,17},{9,1... | collective-permute-start | bytes 147464
  1421.0 40.0 %collective-permute-start.17 = (f32[8,1536]{1,0:T(8,128)S(1)}, f32[8,1536]{1,0:T(8,128)S(1)}, u32[]{:S(2)}, u32[]{:S(2)}) collective-permute-start(f32[8,1536]{1,0:T(8,128)S(1)} %fusion), channel_id=1, source_target_pairs={{0,8},{1,9},{2,10},{3,11},{4,12},{5,13},{6,14},{7,15},{8,16},{9,17... | collective-permute-start | bytes 147464
  1434.1 40.0 %collective-permute-start.16 = (f32[8,1536]{1,0:T(8,128)S(1)}, f32[8,1536]{1,0:T(8,128)S(1)}, u32[]{:S(2)}, u32[]{:S(2)}) collective-permute-start(f32[8,1536]{1,0:T(8,128)S(1)} %fusion), channel_id=1, source_target_pairs={{0,7},{1,8},{2,9},{3,10},{4,11},{5,12},{6,13},{7,14},{8,15},{9,16}... | collective-permute-start | bytes 147464
  1447.3 40.4 %collective-permute-start.15 = (f32[8,1536]{1,0:T(8,128)S(1)}, f32[8,1536]{1,0:T(8,128)}, u32[]{:S(2)}, u32[]{:S(2)}) collective-permute-start(f32[8,1536]{1,0:T(8,128)S(1)} %fusion), channel_id=1, source_target_pairs={{0,6},{1,7},{2,8},{3,9},{4,10},{5,11},{6,12},{7,13},{8,14},{9,15},... | collective-permute-start | bytes 147464
  1461.0 39.8 %collective-permute-start.14 = (f32[8,1536]{1,0:T(8,128)S(1)}, f32[8,1536]{1,0:T(8,128)}, u32[]{:S(2)}, u32[]{:S(2)}) collective-permute-start(f32[8,1536]{1,0:T(8,128)S(1)} %fusion), channel_id=1, source_target_pairs={{0,5},{1,6},{2,7},{3,8},{4,9},{5,10},{6,11},{7,12},{8,13},{9,14},{... | collective-permute-start | bytes 147464
  1474.2 39.8 %collective-permute-start.13 = (f32[8,1536]{1,0:T(8,128)S(1)}, f32[8,1536]{1,0:T(8,128)}, u32[]{:S(2)}, u32[]{:S(2)}) collective-permute-start(f32[8,1536]{1,0:T(8,128)S(1)} %fusion), channel_id=1, source_target_pairs={{0,4},{1,5},{2,6},{3,7},{4,8},{5,9},{6,10},{7,11},{8,12},{9,13},{1... | collective-permute-start | bytes 147464
  1487.7 46.2 %collective-permute-start.12 = (f32[8,1536]{1,0:T(8,128)S(1)}, f32[8,1536]{1,0:T(8,128)}, u32[]{:S(2)}, u32[]{:S(2)}) collective-permute-start(f32[8,1536]{1,0:T(8,128)S(1)} %fusion), channel_id=1, source_target_pairs={{0,3},{1,4},{2,5},{3,6},{4,7},{5,8},{6,9},{7,10},{8,11},{9,12},{10... | collective-permute-start | bytes 147464
  1500.8 33.0 %collective-permute-start.11 = (f32[8,1536]{1,0:T(8,128)S(1)}, f32[8,1536]{1,0:T(8,128)}, u32[]{:S(2)}, u32[]{:S(2)}) collective-permute-start(f32[8,1536]{1,0:T(8,128)S(1)} %fusion), channel_id=1, source_target_pairs={{0,2},{1,3},{2,4},{3,5},{4,6},{5,7},{6,8},{7,9},{8,10},{9,11},{10,... | collective-permute-start | bytes 147464
  1514.0 19.9 %collective-permute-start.10 = (f32[8,1536]{1,0:T(8,128)S(1)}, f32[8,1536]{1,0:T(8,128)}, u32[]{:S(2)}, u32[]{:S(2)}) collective-permute-start(f32[8,1536]{1,0:T(8,128)S(1)} %fusion), channel_id=1, source_target_pairs={{0,1},{1,2},{2,3},{3,4},{4,5},{5,6},{6,7},{7,8},{8,9},{9,10},{10,1... | collective-permute-start | bytes 147464
  (110 other events, 11707.7 us)
Sparse Core Ops, SparseCore 0:
  151.9 197.1 all-gather.3
